TPU v7x, 128 devices: a whole 4x4x4 slice. The times are simulated.
128 devices in a mesh: ex: 16 (over y, z_lo, core), lg: 8 (over x, z_hi).
Axes of the slice: x: 4, y: 4, z: 4 (z_hi: 2, z_lo: 2; z = z_hi * 2 + z_lo), core: 2. Of those that a mesh axis runs over, the one named last changes fastest.
Arguments:
- query_factors: bfloat16 [32, 16, 32, 128, 128], P(None, 'ex', 'lg'), may hold values from -6 to 6
- rewards: float32 [32, 16], replicated, may hold values from -4 to 4
- ranking: int32 [32, 16], replicated, may hold values from 0 to 15, each once within a row
- list_len: int32 [32], replicated, may hold values from 1 to 16
- store_slab: bfloat16 [4096, 32, 4096], P('ex', 'lg')
Outputs:
- scores: float32 [32, 4096], P('lg', 'ex')
Inputs may be any that keep to these rules, and one draw needn't show every extreme that they name: Each row of ranking names every response of its list once.
All inputs are finite; a program needn't handle non-finite values.
Results may differ from a plain program's by a relative error of at most 0.0029.
Values may be sent and summed in bfloat16 or wider, within the bound.
No kernel may reach another device: no remote copies, remote signals or barrier semaphores. Data moves between devices by JAX's collectives and lax.ppermute only.
A program may use at most 64 MiB of HBM per device.

v0:
```python
import jax
import jax.numpy as jnp
from jax import lax
from jax.sharding import PartitionSpec as P

EPS = 1e-06


def list_weights(rewards, ranking, list_len):
    count = rewards.shape[1]
    ordered = jnp.take_along_axis(rewards, ranking, axis=1)
    expo = jnp.exp(ordered)
    tail = jnp.cumsum(expo[:, ::-1], axis=1)[:, ::-1]
    place = jnp.arange(count, dtype=jnp.int32)[None, :]
    active = (place < list_len[:, None]).astype(jnp.float32)
    lead = jnp.cumsum(active / tail, axis=1)
    sorted_w = expo * lead - active
    match = (ranking[:, :, None] == jnp.arange(count, dtype=jnp.int32)[None, None, :]).astype(
        jnp.float32
    )
    return jnp.sum(sorted_w[:, :, None] * match, axis=1)


def per_device(query_factors, rewards, ranking, list_len, store_slab):
    resp_dev = query_factors.shape[1]
    layer_dev = query_factors.shape[2]
    tok_count = query_factors.shape[3]
    rank_dim = query_factors.shape[4] // 2
    query_count = query_factors.shape[0]
    weights = list_weights(rewards, ranking, list_len)
    first_resp = lax.axis_index("ex") * resp_dev
    mine = lax.dynamic_slice_in_dim(weights, first_resp, resp_dev, 1)
    inputs = query_factors[..., :rank_dim]
    outputs = query_factors[..., rank_dim:]
    per_resp = lax.dot_general(
        outputs, inputs, (((3,), (3,)), ((0, 1, 2), (0, 1, 2))), preferred_element_type=jnp.float32
    )
    per_resp = per_resp * tok_count ** (-0.5)
    partial_value = jnp.sum(mine[:, :, None, None, None] * per_resp, axis=1)
    partial_value = partial_value.reshape(query_count, layer_dev * rank_dim * rank_dim)
    qgrad = lax.psum(partial_value, "ex").astype(jnp.bfloat16)
    store_rows = store_slab.shape[0]
    flat_store = store_slab.reshape(store_rows, layer_dev * store_slab.shape[2])
    norm_local = jnp.einsum("nf,nf->n", flat_store, flat_store, preferred_element_type=jnp.float32)
    norm_sq = lax.psum(norm_local, "lg")
    share = lax.psum_scatter(
        lax.dot_general(
            qgrad, flat_store, (((1,), (1,)), ((), ())), preferred_element_type=jnp.float32
        ),
        "lg",
        scatter_dimension=0,
        tiled=True,
    )
    return share * lax.rsqrt(norm_sq + EPS)[None, :]


def solution(mesh):
    placed = (P(None, "ex", "lg", None, None), P(), P(), P(), P("ex", "lg", None))
    return jax.shard_map(
        per_device, mesh=mesh, in_specs=placed, out_specs=P("lg", "ex"), check_vma=False
    )
```

profile of v0, /device:TPU:0, one launch (start us, length us, event | category | flops | bytes accessed | tf_op | source)
XLA Modules:
  0.0 156.2 jit_solution(2549711422795041509)
XLA Ops:
  0.0 0.0 copy-start
  0.0 0.8 copy.26
  0.8 0.1 reshape.61
  0.9 0.0 copy-done
  0.9 0.0 copy-start.3
  0.9 0.0 copy-start.2
  0.9 3.9 %gather_fusion = f32[512]{0:T(512)S(1)} fusion(f32[32,16]{0,1:T(8,128)S(1)} %copy-done, s32[512]{0:T(512)S(1)} %reshape.61), kind=kCustom, calls=%fused_computation | custom fusion | bytes 8192 | tf_op jit(solution)/shard_map/jit(take_along_axis)/gather | solution.py:11
  4.8 0.1 reshape.64
  4.9 0.1 rev.6
  5.0 0.2 reduce_window_sum.17
  5.1 0.1 rev.7
  5.2 0.0 copy-done.3
  5.2 0.1 convert_divide_fusion
  5.3 0.2 reduce_window_sum.18
  5.5 0.1 convert_subtract_fusion
  5.6 0.1 copy.29
  5.6 0.0 copy-done.2
  5.7 8.9 %broadcast_multiply_fusion = f32[32,4,64,64]{3,2,1,0:T(8,128)} fusion(f32[32]{0:T(128)S(1)} %multiply_bitcast_fusion, bf16[32,1,4,128,128]{4,3,2,1,0:T(8,128)(2,1)} %param.5), kind=kOutput, calls=%fused_computation.8 | convolution fusion | flops 134742016 | bytes 10485888 | tf_op jit(solution)/shard_map/dot_general | solution.py:35
  14.6 2.9 %reshape.59 = f32[32,16384]{1,0:T(8,128)S(1)} reshape(f32[32,4,64,64]{3,2,1,0:T(8,128)} %broadcast_multiply_fusion) | data formatting | bytes 4194304 | tf_op jit(solution)/shard_map/reshape | solution.py:40
  17.5 70.7 %all-reduce.3 = bf16[32,16384]{1,0:T(8,128)(2,1)S(1)} all-reduce(f32[32,16384]{1,0:T(8,128)S(1)} %reshape.59), channel_id=1, replica_groups=mesh['ex'=16,'lg'=8] {'ex'}, use_global_device_ids=true, to_apply=%region_3.4 | all-reduce | flops 524288 | bytes 3145728 | tf_op jit(solution)/shard_map/psum | solution.py:41
  88.2 15.5 %copy.36 = bf16[32,8,4,4096]{3,1,2,0:T(8,128)(2,1)} copy(bf16[32,8,4,4096]{3,2,1,0:T(4,128)(2,1)} %bitcast.27) | data formatting | bytes 16777216
  103.7 0.0 copy-start.1
  103.7 6.1 %fusion.12 = f32[32,256]{1,0:T(8,128)S(1)} fusion(bf16[32,16384]{1,0:T(8,128)(2,1)S(1)} %all-reduce.3, bf16[256,16384]{1,0:T(8,128)(2,1)} %bitcast.25), kind=kOutput, calls=%fused_computation.22 | convolution fusion | flops 268435456 | bytes 9469952 | tf_op jit(solution)/shard_map/dot_general | solution.py:47
  109.8 0.0 copy-done.1
  109.8 0.0 copy-start.4
  109.8 1.8 %fusion = f32[256]{0:T(256)S(1)} fusion(bf16[256,16384]{1,0:T(8,128)(2,1)S(1)} %bitcast.26), kind=kLoop, calls=%fused_computation.2 | loop fusion | flops 12582656 | bytes 8389632 | tf_op jit(solution)/shard_map/nf,nf->n/dot_general | solution.py:44
  111.6 42.7 %all-reduce.1 = (f32[32,256]{1,0:T(8,128)S(1)}, f32[256]{0:T(256)S(1)}) all-reduce(f32[32,256]{1,0:T(8,128)S(1)} %fusion.12, f32[256]{0:T(256)S(1)} %fusion), channel_id=2, replica_groups=mesh['ex'=16,'lg'=8] {'lg'}, use_global_device_ids=true, to_apply=%region_4.5.clone | all-reduce | flops 8448 | bytes 67584
  154.3 0.0 copy-done.4
  154.3 0.6 dynamic-slice
  155.6 0.6 dynamic-slice_multiply_fusion
  (5 shorter events, 0.1 us)
Async XLA Ops:
  0.0 0.9 copy-start
  0.9 4.3 %copy-start.3 = (s32[32]{0:T(128)S(1)}, s32[32]{0:T(128)}, u32[]{:S(2)}) copy-start(s32[32]{0:T(128)} %param.8) | copy-start | bytes 388
  0.9 4.7 %copy-start.2 = (s32[32,16]{0,1:T(8,128)S(1)}, s32[32,16]{0,1:T(8,128)}, u32[]{:S(2)}) copy-start(s32[32,16]{0,1:T(8,128)} %param.7) | copy-start | bytes 6148
  103.7 6.2 %copy-start.1 = (bf16[32,8,4,4096]{3,1,2,0:T(8,128)(2,1)S(1)}, bf16[32,8,4,4096]{3,1,2,0:T(8,128)(2,1)}, u32[]{:S(2)}) copy-start(bf16[32,8,4,4096]{3,1,2,0:T(8,128)(2,1)} %copy.36) | copy-start | bytes 25165828
  109.8 44.5 %copy-start.4 = (u32[128]{0:T(128)S(1)}, u32[128]{0:T(128)}, u32[]{:S(2)}) copy-start(u32[128]{0:T(128)} %constant.53) | copy-start | bytes 1540
where the time goes:
time: 156 us
  blocking collectives  113 us (72%)
  local copies, waits for them, and re-layouts  24 us (15%)
  matrix products  15 us (10%)
  other arithmetic  2.94 us (2%)
    psum x1, blocking collectives, per_device(): qgrad = lax.psum(partial_value, 'ex').astype(jnp.bfloat16)  70.7 us
    unnamed x1, blocking collectives  42.7 us
    unnamed x13, local copies, waits for them, and re-layouts  16.9 us
    dot_general x1, matrix products, per_device(): lax.dot_general(outputs, inputs, (((3,), (3,)), ((0, 1, 2), (0, 1, 2))),...  8.86 us
    dot_general x1, matrix products, per_device(): lax.dot_general(qgrad, flat_store, (((1,), (1,)), ((), ())), preferred_el...  6.13 us
    gather x3, local copies, waits for them, and re-layouts, list_weights(): ordered = jnp.take_along_axis(rewards, ranking, axis=1)  4.05 us

commit v1 on v0

v1 whole, which is shorter than its diff:
```python
import jax
import jax.numpy as jnp
from jax import lax
from jax.experimental import pallas as pl
from jax.experimental.pallas import tpu as pltpu
from jax.sharding import PartitionSpec as P

EPS = 1e-06
F32 = jnp.float32
BF16 = jnp.bfloat16
HIGH = lax.Precision.HIGHEST
VMEM = 24 << 20
Q_STEP = 8


def params():
    return pltpu.CompilerParams(vmem_limit_bytes=VMEM)


def whole(shape):
    return pl.BlockSpec(shape, lambda *_: (0,) * len(shape))


def my_weights(rew, rank, length, me):
    count = rew.shape[0]
    ordered = jnp.zeros_like(rew)
    for k in range(count):
        ordered = ordered + jnp.where(rank == k, rew[k : k + 1, :], 0.0)
    expo = jnp.exp(ordered)
    rows = [expo[j : j + 1, :] for j in range(count)]
    tails = [None] * count
    total = None
    for j in reversed(range(count)):
        total = rows[j] if total is None else total + rows[j]
        tails[j] = total
    lead = None
    out = jnp.zeros_like(rows[0])
    for j in range(count):
        active = (length > j).astype(F32)
        term = active / tails[j]
        lead = term if lead is None else lead + term
        out = out + jnp.where(rank[j : j + 1, :] == me, rows[j] * lead - active, 0.0)
    return out


def outer_kernel(x_ref, rew_ref, rank_ref, len_ref, mine_ref, other_ref, w_ref, m_ref):
    queries = rew_ref.shape[1]
    layers = x_ref.shape[1]
    tokens = x_ref.shape[2]
    half = x_ref.shape[3] // 2
    lanes = 2 * half
    step_rows = layers * Q_STEP
    ex = lax.axis_index("ex")
    core = lax.rem(ex, 2)
    step = pl.program_id(0)

    @pl.when(step == 0)
    def _():
        w = my_weights(rew_ref[...], rank_ref[...], len_ref[...], ex) * tokens ** (-0.5)
        at = lax.broadcasted_iota(jnp.int32, (queries, queries), 0)
        to = lax.broadcasted_iota(jnp.int32, (queries, queries), 1)
        column = jnp.sum(jnp.where(at == to, w, 0.0), axis=1, keepdims=True)
        w_ref[...] = jnp.broadcast_to(column, w_ref.shape)

    for q in range(Q_STEP):
        w = w_ref[pl.ds(step * Q_STEP + q, 1), :]
        for layer in range(layers):
            x = x_ref[q, layer]
            inp = x[:, :half]
            twice = jnp.concatenate([inp, inp], axis=1)
            m = lax.dot_general(
                x[:, half:], twice, (((0,), (0,)), ((), ())), preferred_element_type=F32
            )
            m_ref[pl.ds(layer * Q_STEP + q, half, stride=step_rows), :] = m * w
    low = lax.broadcasted_iota(jnp.int32, (step_rows, lanes), 1) < half
    for which, ref in ((core, mine_ref), (1 - core, other_ref)):
        for piece in range(ref.shape[0]):
            for t in range(2):
                row = (which * (half // 2) + 4 * piece + 2 * t) * step_rows
                even = m_ref[pl.ds(pl.multiple_of(row, step_rows), step_rows), :]
                odd = m_ref[pl.ds(pl.multiple_of(row + step_rows, step_rows), step_rows), :]
                both = jnp.where(low, even, odd).reshape(layers, Q_STEP, lanes)
                ref[piece, :, :, t * lanes : (t + 1) * lanes] = both


def outer(factors, rew, rank, length, chips):
    queries, layers, tokens, lanes = factors.shape
    half = lanes // 2
    part = (chips, layers, queries, 2 * lanes)
    block = (chips, layers, Q_STEP, 2 * lanes)
    return pl.pallas_call(
        outer_kernel,
        grid=(queries // Q_STEP,),
        in_specs=[
            pl.BlockSpec((Q_STEP, layers, tokens, lanes), lambda i: (i, 0, 0, 0)),
            whole(rew.shape),
            whole(rank.shape),
            whole(length.shape),
        ],
        out_specs=[pl.BlockSpec(block, lambda i: (0, 0, i, 0))] * 2,
        out_shape=[jax.ShapeDtypeStruct(part, F32)] * 2,
        scratch_shapes=[
            pltpu.VMEM((queries, lanes), F32),
            pltpu.VMEM((half * layers * Q_STEP, lanes), F32),
        ],
        compiler_params=params(),
        name="outer",
    )(factors, rew, rank, length)


def pair_kernel(mine_ref, got_ref, send_ref, own_ref):
    chip = lax.div(lax.axis_index("ex"), 2)
    for s in range(mine_ref.shape[0]):
        send_ref[s] = (mine_ref[s] + got_ref[s]).astype(BF16)
    own_ref[...] = mine_ref[chip] + got_ref[chip]


def pair(mine, got):
    return pl.pallas_call(
        pair_kernel,
        in_specs=[whole(mine.shape)] * 2,
        out_specs=[whole(mine.shape), whole(mine.shape[1:])],
        grid=(1,),
        out_shape=[
            jax.ShapeDtypeStruct(mine.shape, BF16),
            jax.ShapeDtypeStruct(mine.shape[1:], F32),
        ],
        compiler_params=params(),
        name="pair",
    )(mine, got)


def total_kernel(own_ref, got_ref, out_ref):
    chip = lax.div(lax.axis_index("ex"), 2)
    total = own_ref[...]
    for s in range(got_ref.shape[0]):
        total = total + jnp.where(chip == s, 0.0, got_ref[s].astype(F32))
    total = total.astype(BF16)
    for s in range(out_ref.shape[0]):
        out_ref[s] = total


def total(own, got):
    return pl.pallas_call(
        total_kernel,
        in_specs=[whole(own.shape), whole(got.shape)],
        out_specs=whole(got.shape),
        grid=(1,),
        out_shape=jax.ShapeDtypeStruct(got.shape, BF16),
        compiler_params=params(),
        name="total",
    )(own, got)


def relay_kernel(x_ref, s_ref, n_ref):
    rows, layers, width = x_ref.shape
    depth = s_ref.shape[2]
    v = x_ref[...].reshape(rows * layers, width)
    for g in range(width // depth):
        s_ref[g] = v[:, g * depth : (g + 1) * depth]
    f = v.astype(F32)
    acc = None
    for c in range(width // 128):
        t = f[:, c * 128 : (c + 1) * 128]
        acc = t * t if acc is None else acc + t * t
    acc = jnp.sum(acc.reshape(rows, layers, 128), axis=1)
    n_ref[...] = lax.dot_general(
        jnp.ones((8, 128), F32),
        acc,
        (((1,), (1,)), ((), ())),
        precision=HIGH,
        preferred_element_type=F32,
    )


def relay(store, depth, block=128):
    rows, layers, width = store.shape
    parts = width // depth
    return pl.pallas_call(
        relay_kernel,
        grid=(rows // block,),
        in_specs=[pl.BlockSpec((block, layers, width), lambda i: (i, 0, 0))],
        out_specs=[
            pl.BlockSpec((parts, block * layers, depth), lambda i: (0, i, 0)),
            pl.BlockSpec((8, block), lambda i: (0, i)),
        ],
        out_shape=[
            jax.ShapeDtypeStruct((parts, rows * layers, depth), BF16),
            jax.ShapeDtypeStruct((8, rows), F32),
        ],
        compiler_params=params(),
        cost_estimate=pl.CostEstimate(flops=64 << 20, bytes_accessed=40 << 20, transcendentals=0),
        name="relay",
    )(store)


def score_kernel(s_ref, own_ref, got_ref, n_ref, out_ref, g_ref):
    layers = own_ref.shape[1]
    queries = own_ref.shape[2]
    rows = s_ref.shape[1] // layers
    chips = own_ref.shape[0]
    core = lax.rem(lax.axis_index("ex"), 2)
    step = pl.program_id(0)

    @pl.when(step == 0)
    def _():
        g_ref[...] = jnp.zeros_like(g_ref)

    def add(ref, piece):
        q = ref[piece].reshape(layers * queries, ref.shape[3])
        g_ref[...] += lax.dot_general(
            s_ref[0], q, (((1,), (1,)), ((), ())), preferred_element_type=F32
        )

    piece = lax.rem(step, chips)
    own = lax.div(step, chips) == core

    @pl.when(own)
    def _():
        add(own_ref, piece)

    @pl.when(jnp.logical_not(own))
    def _():
        add(got_ref, piece)

    @pl.when(step == pl.num_programs(0) - 1)
    def _():
        g = g_ref[...]
        at = lax.rem(lax.broadcasted_iota(jnp.int32, g.shape, 0), layers)
        to = lax.div(lax.broadcasted_iota(jnp.int32, g.shape, 1), queries)
        g = jnp.where(at == to, g, 0.0)
        g = jnp.sum(g.reshape(rows, layers, layers * queries), axis=1)
        row = lax.broadcasted_iota(jnp.int32, (queries, layers * queries), 0)
        col = lax.rem(lax.broadcasted_iota(jnp.int32, (queries, layers * queries), 1), queries)
        pick = jnp.where(row == col, 1.0, 0.0).astype(F32)
        scores = lax.dot_general(
            pick, g, (((1,), (1,)), ((), ())), precision=HIGH, preferred_element_type=F32
        )
        each = queries // out_ref.shape[0]
        for j in range(out_ref.shape[0]):
            out_ref[j, :each, :] = scores[j * each : (j + 1) * each, :]
            out_ref[j, each:, :] = n_ref[: 8 - each, :]


def score(packed, own, got, norms, groups):
    parts, rows, depth = packed.shape
    layers, queries = own.shape[1:3]
    return pl.pallas_call(
        score_kernel,
        grid=(parts,),
        in_specs=[
            pl.BlockSpec((1, rows, depth), lambda i: (i, 0, 0)),
            whole(own.shape),
            whole(got.shape),
            whole(norms.shape),
        ],
        out_specs=whole((groups, 8, rows // layers)),
        out_shape=jax.ShapeDtypeStruct((groups, 8, rows // layers), F32),
        scratch_shapes=[pltpu.VMEM((rows, layers * queries), F32)],
        compiler_params=params(),
        name="score",
    )(packed, own, got, norms)


def last_kernel(got_ref, out_ref):
    each = out_ref.shape[0]
    total = got_ref[0]
    for s in range(1, got_ref.shape[0]):
        total = total + got_ref[s]
    out_ref[...] = total[:each, :] * lax.rsqrt(total[each : each + 1, :] + EPS)


def last(got, each):
    return pl.pallas_call(
        last_kernel,
        in_specs=[whole(got.shape)],
        out_specs=whole((each, got.shape[2])),
        grid=(1,),
        out_shape=jax.ShapeDtypeStruct((each, got.shape[2]), F32),
        compiler_params=params(),
        name="last",
    )(got)


def solution(mesh):
    ex, lg = mesh.shape["ex"], mesh.shape["lg"]
    chips = ex // 2
    same_core = [[2 * i + c for i in range(chips)] for c in range(2)]
    twin = [(i, i ^ 1) for i in range(ex)]

    def per_device(query_factors, rewards, ranking, list_len, store_slab):
        queries, _, layers, tokens, lanes = query_factors.shape
        factors = query_factors.reshape(queries, layers, tokens, lanes)
        mine, other = outer(factors, rewards.T, ranking.T, list_len[None, :], chips)
        got = lax.ppermute(other, "ex", twin)
        send, own = pair(mine, got)
        packed, norms = relay(store_slab, 2 * lanes)
        got = lax.all_to_all(send, "ex", 0, 0, axis_index_groups=same_core)
        summed = total(own, got)
        held = lax.all_to_all(summed, "ex", 0, 0, axis_index_groups=same_core)
        got = lax.ppermute(held, "ex", twin)
        partial = score(packed, held, got, norms, lg)
        got = lax.all_to_all(partial, "lg", 0, 0)
        return last(got, queries // lg)

    placed = (P(None, "ex", "lg", None, None), P(), P(), P(), P("ex", "lg", None))
    return jax.shard_map(
        per_device, mesh=mesh, in_specs=placed, out_specs=P("lg", "ex"), check_vma=False
    )
```

time: 156 us -> 76.9 us (0.49)
  blocking collectives: 113 us -> 42.8 us
  Pallas kernels: 0 us -> 26.2 us
  local copies, waits for them, and re-layouts: 24 us -> 4.89 us
  matrix products: 15 us -> 0 us
  other arithmetic: 2.94 us -> 0 us
  waiting for transfers between devices: 0 us -> 2.65 us
    psum x1 -> x0, blocking collectives: 70.7 us -> none  [per_device(): qgrad = lax.psum(partial_value, 'ex').astype(jnp.bfloat16)]
    all_to_all x0 -> x3, blocking collectives: none -> 42.8 us  [the longest x1 15.7 us: per_device(): got = lax.all_to_all(send, 'ex', 0, 0, axis_index_groups=same_core)]
    unnamed x1 -> x0, blocking collectives: 42.7 us -> none
    pallas_call x0 -> x6, Pallas kernels: none -> 26.2 us  [the longest x1 11 us: relay(): pl.pallas_call(relay_kernel, grid=(rows // block,), in_specs=[pl.BlockSpe...]
    dot_general x2 -> x0, matrix products: 15 us -> none  [the longest x1 8.86 us: per_device(): lax.dot_general(outputs, inputs, (((3,), (3,)), ((0, 1, 2), (0, 1, 2))),...]
    unnamed x13 -> x10, local copies, waits for them, and re-layouts: 16.9 us -> 4.89 us
    gather x3 -> x0, local copies, waits for them, and re-layouts: 4.05 us -> none  [list_weights(): ordered = jnp.take_along_axis(rewards, ranking, axis=1)]
    reshape x1 -> x0, local copies, waits for them, and re-layouts: 2.91 us -> none  [per_device(): partial_value.reshape(query_count, layer_dev * rank_dim * rank_dim)]
  transfers between devices with their start and end apart: 0 -> 2, of which waited for: 0 -> 1; matrix products, arithmetic and copies ran while one was open for 0% -> 0% of each run, Pallas kernels for 0% -> 14%
where the time goes in v1:
time: 76.9 us; the launch traced here: 76.6 us
  blocking collectives  42.8 us (56%)
  Pallas kernels  26.2 us (34%)
  local copies, waits for them, and re-layouts  4.89 us (6%)
  waiting for transfers between devices  2.65 us (3%)
    all_to_all x1, blocking collectives, per_device(): got = lax.all_to_all(send, 'ex', 0, 0, axis_index_groups=same_core)  15.7 us
    all_to_all x1, blocking collectives, per_device(): got = lax.all_to_all(partial, 'lg', 0, 0)  15 us
    all_to_all x1, blocking collectives, per_device(): held = lax.all_to_all(summed, 'ex', 0, 0, axis_index_groups=same_core)  12.1 us
    pallas_call x1, Pallas kernels, relay(): pl.pallas_call(relay_kernel, grid=(rows // block,), in_specs=[pl.BlockSpe...  11 us
    pallas_call x1, Pallas kernels, outer(): pl.pallas_call(outer_kernel, grid=(queries // Q_STEP,), in_specs=[pl.Bloc...  8.57 us
    pallas_call x1, Pallas kernels, score(): pl.pallas_call(score_kernel, grid=(parts,), in_specs=[pl.BlockSpec((1, ro...  5.72 us
    unnamed x10, local copies, waits for them, and re-layouts  4.89 us
    ppermute x1, waiting for transfers between devices, per_device(): got = lax.ppermute(other, 'ex', twin)  2.65 us
  transfers between devices with their start and end apart: 2, of which 1 were waited for; matrix products, arithmetic and copies ran while one was open for 0% of the time, Pallas kernels for 14%

profile of v1, /device:TPU:0, one launch (start us, length us, event | category | flops | bytes accessed | tf_op | source)
XLA Modules:
  0.0 76.6 jit_solution(7677941888367118144)
XLA Ops:
  0.0 0.0 copy-start
  0.0 0.0 copy-start.1
  0.0 2.3 %copy-done.1 = bf16[32,1,4,128,128]{4,3,2,1,0:T(8,128)(2,1)S(1)} copy-done((bf16[32,1,4,128,128]{4,3,2,1,0:T(8,128)(2,1)S(1)}, bf16[32,1,4,128,128]{4,3,2,1,0:T(8,128)(2,1)}, u32[]{:S(2)}) %copy-start.1) | copy-done | bytes 4194328
  2.3 0.0 copy-start.2
  2.3 0.9 %copy-done.2 = f32[32,16]{0,1:T(8,128)S(1)} copy-done((f32[32,16]{0,1:T(8,128)S(1)}, f32[32,16]{0,1:T(8,128)}, u32[]{:S(2)}) %copy-start.2) | copy-done | bytes 2072
  3.3 0.0 copy-start.3
  3.3 1.0 %copy-done.3 = s32[32,16]{0,1:T(8,128)S(1)} copy-done((s32[32,16]{0,1:T(8,128)S(1)}, s32[32,16]{0,1:T(8,128)}, u32[]{:S(2)}) %copy-start.3) | copy-done | bytes 2072
  4.2 0.0 copy-start.4
  4.2 0.7 copy-done.4
  4.9 8.6 %outer.1 = (f32[8,4,32,256]{3,2,1,0:T(8,128)S(1)}, f32[8,4,32,256]{3,2,1,0:T(8,128)S(1)}) custom-call(bf16[32,4,128,128]{3,2,1,0:T(8,128)(2,1)S(1)} %bitcast.4, f32[16,32]{1,0:T(8,128)S(1)} %bitcast.5, s32[16,32]{1,0:T(8,128)S(1)} %bitcast.6, s32[1,32]{1,0:T(1,128)S(1)} %bitcast.7), custom_call_target="tpu_custom_call" | custom-call | tf_op jit(solution)/shard_map/outer/pallas_call | solution.py:91
  13.5 0.1 collective-permute-start
  13.6 2.6 %collective-permute-done.got_ref = f32[8,4,32,256]{3,2,1,0:T(8,128)S(1)} collective-permute-done((f32[8,4,32,256]{3,2,1,0:T(8,128)S(1)}, f32[8,4,32,256]{3,2,1,0:T(8,128)S(1)}, u32[]{:S(2)}, u32[]{:S(2)}) %collective-permute-start) | collective-permute-done | bytes 1048608 | tf_op jit(solution)/shard_map/ppermute | solution.py:295
  16.2 0.1 pair.1
  16.3 15.7 %all_to_all.15.got_ref = bf16[8,4,32,256]{3,2,1,0:T(8,128)(2,1)S(1)} all-to-all(bf16[8,4,32,256]{3,2,1,0:T(8,128)(2,1)S(1)} %get-tuple-element.15), channel_id=1, replica_groups={{0,16,32,48,64,80,96,112},{8,24,40,56,72,88,104,120},{1,17,33,49,65,81,..., dimensions={0} | all-to-all | bytes 1048576 | tf_op jit(solution)/shard_map/all_to_all | solution.py:298
  32.1 0.1 total.1
  32.2 12.1 %all_to_all.16.own_ref = bf16[8,4,32,256]{3,2,1,0:T(8,128)(2,1)S(1)} all-to-all(bf16[8,4,32,256]{3,2,1,0:T(8,128)(2,1)S(1)} %total.1), channel_id=1, replica_groups={{0,16,32,48,64,80,96,112},{8,24,40,56,72,88,104,120},{1,17,33,49,65,81,..., dimensions={0} | all-to-all | bytes 1048576 | tf_op jit(solution)/shard_map/all_to_all | solution.py:300
  44.3 0.0 collective-permute-start.1
  44.3 0.0 copy-done
  44.3 11.0 %relay.1 = (bf16[16,1024,256]{2,1,0:T(8,128)(2,1)S(1)}, f32[8,256]{1,0:T(8,128)S(1)}) custom-call(bf16[256,4,4096]{2,1,0:T(4,128)(2,1)S(1)} %copy-done), custom_call_target="tpu_custom_call" | custom-call | flops 67108864 | bytes 41943040 | tf_op jit(solution)/shard_map/relay/pallas_call | solution.py:179
  55.3 0.0 collective-permute-done.1.got_ref
  55.4 5.7 %score.1 = f32[8,8,256]{2,1,0:T(8,128)S(1)} custom-call(bf16[16,1024,256]{2,1,0:T(8,128)(2,1)S(1)} %get-tuple-element.11.s_ref, bf16[8,4,32,256]{3,2,1,0:T(8,128)(2,1)S(1)} %all_to_all.16.own_ref, bf16[8,4,32,256]{3,2,1,0:T(8,128)(2,1)S(1)} %collective-permute-done.1.got_ref, f32[8,256]{1,0:T(8,128)S(1)} %get-tuple-element.16.n_ref), custom_call_target="tpu_custom_call" | custom-call | tf_op jit(solution)/shard_map/score/pallas_call | solution.py:248
  61.1 15.0 %all_to_all.17.got_ref = f32[8,8,256]{2,1,0:T(8,128)S(1)} all-to-all(f32[8,8,256]{2,1,0:T(8,128)S(1)} %score.1), channel_id=1, replica_groups=mesh['ex'=16,'lg'=8] {'lg'}, dimensions={0} | all-to-all | bytes 131072 | tf_op jit(solution)/shard_map/all_to_all | solution.py:303
  76.0 0.6 last.1
Async XLA Ops:
  0.0 44.3 %copy-start = (bf16[256,4,4096]{2,1,0:T(4,128)(2,1)S(1)}, bf16[256,4,4096]{2,1,0:T(4,128)(2,1)}, u32[]{:S(2)}) copy-start(bf16[256,4,4096]{2,1,0:T(4,128)(2,1)} %x_ref.1) | copy-start | bytes 25165828
  0.0 2.3 %copy-start.1 = (bf16[32,1,4,128,128]{4,3,2,1,0:T(8,128)(2,1)S(1)}, bf16[32,1,4,128,128]{4,3,2,1,0:T(8,128)(2,1)}, u32[]{:S(2)}) copy-start(bf16[32,1,4,128,128]{4,3,2,1,0:T(8,128)(2,1)} %param.5) | copy-start | bytes 12582916
  2.3 0.9 %copy-start.2 = (f32[32,16]{0,1:T(8,128)S(1)}, f32[32,16]{0,1:T(8,128)}, u32[]{:S(2)}) copy-start(f32[32,16]{0,1:T(8,128)} %param.6) | copy-start | bytes 6148
  3.3 1.0 %copy-start.3 = (s32[32,16]{0,1:T(8,128)S(1)}, s32[32,16]{0,1:T(8,128)}, u32[]{:S(2)}) copy-start(s32[32,16]{0,1:T(8,128)} %param.7) | copy-start | bytes 6148
  4.2 0.7 copy-start.4
  13.5 2.7 %collective-permute-start = (f32[8,4,32,256]{3,2,1,0:T(8,128)S(1)}, f32[8,4,32,256]{3,2,1,0:T(8,128)S(1)}, u32[]{:S(2)}, u32[]{:S(2)}) collective-permute-start(f32[8,4,32,256]{3,2,1,0:T(8,128)S(1)} %get-tuple-element.13), channel_id=1, source_target_pairs={{0,8},{8,0},{16,24},{24,16},{32,40},{40,32},{48,56},{56,48},{64,72... | collective-permute-start | bytes 3145736 | tf_op jit(solution)/shard_map/ppermute | solution.py:295
  44.3 11.1 %collective-permute-start.1 = (bf16[8,4,32,256]{3,2,1,0:T(8,128)(2,1)S(1)}, bf16[8,4,32,256]{3,2,1,0:T(8,128)(2,1)S(1)}, u32[]{:S(2)}, u32[]{:S(2)}) collective-permute-start(bf16[8,4,32,256]{3,2,1,0:T(8,128)(2,1)S(1)} %all_to_all.16.own_ref), channel_id=1, source_target_pairs={{0,8},{8,0},{16,24},{24,16},{32,40},{40,32},{48,56},{56,48},{64,72... | collective-permute-start | bytes 1572872 | tf_op jit(solution)/shard_map/ppermute | solution.py:301
